TPU v7x, 256 devices: a whole 4x4x8 slice. The times are simulated.
256 devices in a mesh: ctx: 32 (over y, x, core), head: 8 (over z).
Axes of the slice: x: 4, y: 4, z: 8, core: 2. Of those that a mesh axis runs over, the one named last changes fastest.
Arguments:
- queries: bfloat16 [32, 4096, 128], P('head', 'ctx'), may hold values from -6 to 6
- keys: bfloat16 [32, 4096, 128], P('head', 'ctx'), may hold values from -6 to 6
- values_in: bfloat16 [32, 4096, 128], P('head', 'ctx'), may hold values from -6 to 6
- out_grad: bfloat16 [32, 4096, 128], P('head', 'ctx'), may hold values from -1.5 to 1.5
- logged_keep_factor: float32 [32, 4096, 128], P('head', 'ctx'), may hold values from -0.75 to 0
- beta: float32 [32, 4096], P('head', 'ctx'), may hold values from 0.1 to 0.95
- conv_weight: float32 [4, 32, 128], P(None, 'head'), may hold values from -2 to 2
Outputs:
- query_grad: float32 [32, 4096, 128], P('head', 'ctx')
- input_grad: float32 [32, 4096, 128], P('head', 'ctx')
All inputs are finite; a program needn't handle non-finite values.
Results may differ from a plain program's by a relative error of at most 0.0003.
Values may be sent and summed in bfloat16 or wider, within the bound.
A program may use at most 128 MiB of HBM per device.

v0:
```python
import jax
import jax.numpy as jnp
from jax import lax
from jax.sharding import PartitionSpec as P

GROUP = 128


highest = lax.Precision.HIGHEST


def shifted(value, axis, steps):
    count = lax.axis_size(axis)
    initial, last = (max(0, -steps), min(count, count - steps))
    return lax.ppermute(value, axis, [(source, source + steps) for source in range(initial, last)])


def prefix(part, axis, combine, identity, reverse):
    count = lax.axis_size(axis)
    place = lax.axis_index(axis)
    ahead = count - 1 - place if reverse else place
    gathered = jax.tree.map(lambda a: lax.all_gather(a, axis), part)
    state = jax.tree.map(lambda a, e: jnp.zeros_like(a) + jnp.asarray(e, a.dtype), part, identity)

    def one(turn, state):
        source = count - 1 - turn if reverse else turn
        return combine(
            state, jax.tree.map(lambda a: lax.dynamic_index_in_dim(a, source, 0, False), gathered)
        )

    return lax.fori_loop(0, ahead, one, state)


def normalize(array):
    scaled = array.astype(jnp.float32)
    return scaled * lax.rsqrt(jnp.sum(scaled * scaled, axis=-1, keepdims=True) + 1e-06)


def apply_left(matrix, other):
    return jnp.einsum("hij,hjk->hik", matrix, other, precision=highest)


def apply_transposed(matrix, other):
    return jnp.einsum("hji,hjk->hik", matrix, other, precision=highest)


def compose(earlier, later):
    return (apply_left(later[0], earlier[0]), apply_left(later[0], earlier[1]) + later[1])


def triangular(system, right, transpose_flag):
    return jax.scipy.linalg.solve_triangular(
        system, right, trans=transpose_flag, lower=True, unit_diagonal=True
    )


def local(queries, keys, values_in, out_grad, logged_keep_factor, beta, conv_weight):
    head_count, token_count, key_width = queries.shape
    conv_taps = conv_weight.shape[0]
    block_length_total = GROUP
    block_count = token_count // block_length_total
    rim = shifted(values_in[:, token_count - conv_taps + 1 :, :], "ctx", 1)
    padded = jnp.concatenate([rim, values_in], axis=1).astype(jnp.float32)
    pre_act = conv_weight[0][:, None, :] * padded[:, conv_taps - 1 : conv_taps - 1 + token_count, :]
    for tap in range(1, conv_taps):
        pre_act = (
            pre_act
            + conv_weight[tap][:, None, :]
            * padded[:, conv_taps - 1 - tap : conv_taps - 1 - tap + token_count, :]
        )
    sigmoid_pre = jax.nn.sigmoid(pre_act)
    value = pre_act * sigmoid_pre

    def blocked(array):
        return array.reshape(head_count, block_count, block_length_total, key_width)

    query_unit = blocked(normalize(queries))
    key_unit = blocked(normalize(keys))
    out_block = blocked(out_grad.astype(jnp.float32))
    value_block = blocked(value)
    gate_block = blocked(logged_keep_factor)
    strength = beta.reshape(head_count, block_count, block_length_total)
    rows_iota = lax.broadcasted_iota(jnp.int32, (block_length_total, block_length_total), 0)
    cols_iota = lax.broadcasted_iota(jnp.int32, (block_length_total, block_length_total), 1)
    lower_ones = (rows_iota >= cols_iota).astype(jnp.float32)
    strict_lower = (rows_iota > cols_iota).astype(jnp.float32)
    upper_ones = (cols_iota >= rows_iota).astype(jnp.float32)
    identity_block = jnp.eye(block_length_total, dtype=jnp.float32)
    identity_width = jnp.eye(key_width, dtype=jnp.float32)
    log_decay = jnp.einsum("ts,hnsd->hntd", lower_ones, gate_block, precision=highest)
    decay = jnp.exp(log_decay)
    growth = jnp.exp(-log_decay)
    final_fading = log_decay[:, :, block_length_total - 1 :, :]
    to_end = jnp.exp(final_fading - log_decay)
    block_decay = jnp.exp(final_fading[:, :, 0, :])
    key_decay = key_unit * decay
    key_growth = key_unit * growth
    key_to_end = key_unit * to_end
    query_decay = query_unit * decay
    lower_mix = (
        jnp.einsum("hntd,hnsd->hnts", key_decay, key_growth, precision=highest)
        * strength[:, :, None, :]
        * strict_lower
    )
    system = identity_block + lower_mix
    solved_keys = triangular(system, key_decay, 0)
    solved_values = triangular(system, value_block, 0)
    weighted_end = key_to_end * strength[..., None]
    transition = block_decay[..., :, None] * identity_width - jnp.einsum(
        "hntc,hntd->hncd", weighted_end, solved_keys, precision=highest
    )
    offset = jnp.einsum("hntc,hntd->hncd", weighted_end, solved_values, precision=highest)
    upper_mix = (
        jnp.einsum("hntd,hnsd->hnts", key_growth, query_decay, precision=highest) * upper_ones
    )
    local_rhs = strength[..., None] * jnp.einsum(
        "hnts,hnsd->hntd", upper_mix, out_block, precision=highest
    )
    local_grad = triangular(system, local_rhs, 1)
    local_carry = jnp.einsum(
        "hntc,hntd->hncd", query_decay, out_block, precision=highest
    ) - jnp.einsum("hntc,hntd->hncd", key_decay, local_grad, precision=highest)
    identity_stack = jnp.broadcast_to(identity_width, (head_count, key_width, key_width))
    zero_stack = jnp.zeros((head_count, key_width, key_width), jnp.float32)
    dev_transition = identity_stack
    dev_offset = zero_stack
    block = 0
    dev_offset = apply_left(transition[:, block], dev_offset) + offset[:, block]
    dev_transition = apply_left(transition[:, block], dev_transition)
    dev_carry = zero_stack
    for block in reversed(range(block_count)):
        dev_carry = apply_transposed(transition[:, block], dev_carry) + local_carry[:, block]
    state_in = prefix(
        (dev_transition, dev_offset), "ctx", compose, (identity_stack, zero_stack), False
    )[1]
    grad_in = prefix(
        (jnp.swapaxes(dev_transition, 1, 2), dev_carry),
        "ctx",
        compose,
        (identity_stack, zero_stack),
        True,
    )[1]
    block = 0
    starts = [state_in]
    start_states = jnp.stack(starts, axis=1)
    ends = [zero_stack] * block_count
    for block in reversed(range(block_count)):
        ends[block] = grad_in
    end_carries = jnp.stack(ends, axis=1)
    deltas = solved_values - jnp.einsum(
        "hntc,hncd->hntd", solved_keys, start_states, precision=highest
    )
    products = (
        jnp.einsum("hntd,hnsd->hnts", out_block, deltas, precision=highest)
        * lower_ones
        * strength[:, :, None, :]
    )
    query_grad = decay * (
        jnp.einsum("hnts,hnsc->hntc", products, key_growth, precision=highest)
        + jnp.einsum("hncd,hntd->hntc", start_states, out_block, precision=highest)
    )
    carry_rhs = strength[..., None] * jnp.einsum(
        "hntc,hncd->hntd", key_to_end, end_carries, precision=highest
    )
    value_grad = local_grad + triangular(system, carry_rhs, 1)
    pre_grad = (
        value_grad.reshape(head_count, token_count, key_width)
        * sigmoid_pre
        * (1.0 + pre_act * (1.0 - sigmoid_pre))
    )
    following = shifted(pre_grad[:, : conv_taps - 1, :], "ctx", -1)
    extended = jnp.concatenate([pre_grad, following], axis=1)
    input_grad = conv_weight[0][:, None, :] * extended[:, 0:token_count, :]
    for tap in range(1, conv_taps):
        input_grad = (
            input_grad + conv_weight[tap][:, None, :] * extended[:, tap : tap + token_count, :]
        )
    return (query_grad.reshape(head_count, token_count, key_width), input_grad)


def solution(mesh):
    in_specs = (
        P("head", "ctx", None),
        P("head", "ctx", None),
        P("head", "ctx", None),
        P("head", "ctx", None),
        P("head", "ctx", None),
        P("head", "ctx"),
        P(None, "head", None),
    )
    out_specs = (P("head", "ctx", None), P("head", "ctx", None))
    return jax.shard_map(local, mesh=mesh, in_specs=in_specs, out_specs=out_specs, check_vma=False)
```

profile of v0, /device:TPU:31, one launch (start us, length us, event | category | flops | bytes accessed | tf_op | source)
XLA Modules:
  0.0 359.4 jit_solution(6989643355140289540)
XLA Ops:
  9.6 1.8 fusion.23
  11.3 39.3 %custom-call.8 = f32[4,1,128,128]{2,3,1,0:T(8,128)S(1)} custom-call(f32[4,1,128,128]{3,2,1,0:T(8,128)S(1)} %fusion.23), custom_call_target="InvertDiagBlocksLowerTriangular" | custom-call | tf_op jit(solution)/shard_map/jit(_solve_triangular)/vmap()/triangular_solve | solution.py:52
  50.7 1.6 fusion.52
  52.3 1.7 convolution_subtract_fusion.1
  55.6 1.7 convolution_multiply_fusion.2
  57.4 1.5 fusion.68
  60.4 2.3 fusion.6
  66.6 1.6 collective-permute-done
  68.9 1.5 convolution_add_fusion.2
  70.4 51.6 %all-gather.15.cloned.1.call-done = f32[128,128,128]{2,1,0:T(8,128)} async-done(((f32[4,128,128]{2,1,0:T(8,128)}), f32[128,128,128]{2,1,0:T(8,128)}) %all-gather.15.cloned.1.call-update) | async-done | bytes 8388624 | tf_op jit(solution)/shard_map/all_gather | solution.py:22
  122.0 60.2 %all-gather.13.cloned.1.call-done = f32[128,128,128]{2,1,0:T(8,128)} async-done(((f32[4,128,128]{2,1,0:T(8,128)}), f32[128,128,128]{2,1,0:T(8,128)}) %all-gather.13.cloned.1.call-update) | async-done | bytes 8388624 | tf_op jit(solution)/shard_map/all_gather | solution.py:22
  183.1 3.6 %collective-permute-start.1 = (f32[4,3,128]{2,1,0:T(4,128)S(1)}, f32[4,3,128]{2,1,0:T(4,128)S(1)}, u32[]{:S(2)}, u32[]{:S(2)}) collective-permute-start(f32[4,3,128]{2,1,0:T(4,128)S(1)} %slice.73), channel_id=1, source_target_pairs={{8,0},{16,8},{24,16},{32,24},{40,32},{48,40},{56,48},{64,56},{72,6... | collective-permute-start | bytes 18440 | tf_op jit(solution)/shard_map/ppermute | solution.py:15
  186.8 56.1 %all-gather.9.cloned.1.call-done = f32[128,128,128]{2,1,0:T(8,128)} async-done(((f32[4,128,128]{2,1,0:T(8,128)}), f32[128,128,128]{2,1,0:T(8,128)}) %all-gather.9.cloned.1.call-update) | async-done | bytes 8388624 | tf_op jit(solution)/shard_map/all_gather | solution.py:22
  242.9 60.6 %all-gather.11.cloned.1.call-done = f32[128,128,128]{2,1,0:T(8,128)} async-done(((f32[4,128,128]{2,1,0:T(8,128)}), f32[128,128,128]{2,1,0:T(8,128)}) %all-gather.11.cloned.1.call-update) | async-done | bytes 8388624 | tf_op jit(solution)/shard_map/all_gather | solution.py:22
  303.5 46.2 %while.26 = (s32[]{:T(128)}, f32[4,128,128]{2,1,0:T(8,128)S(1)}, s32[]{:T(128)}, f32[32,4,128,128]{3,2,1,0:T(8,128)}, f32[32,4,128,128]{3,2,1,0:T(8,128)}, /*index=5*/s32[]{:T(128)}, s32[]{:T(128)}, s32[]{:T(128)}) while((s32[]{:T(128)}, f32[4,128,128]{2,1,0:T(8,128)S(1)}, s32[]{:T(128)}, f32[32,4,128,128]{3,2,1,0:T(8,128)}, ...), condition=%wide.region_2.4_spmd, body=%wide.region_1.3_spmd.sunk | while | flops 100728832 | bytes 1574007 | solution.py:31
  303.5 1.4 convolution_add_fusion.5
  305.0 1.4 convolution_add_fusion.5
  306.5 1.4 convolution_add_fusion.5
  309.5 1.4 convolution_add_fusion.5
  311.0 1.4 convolution_add_fusion.5
  312.5 1.4 convolution_add_fusion.5
  313.9 1.4 convolution_add_fusion.5
  316.9 1.4 convolution_add_fusion.5
  318.4 1.4 convolution_add_fusion.5
  319.9 1.4 convolution_add_fusion.5
  321.4 1.4 convolution_add_fusion.5
  324.4 1.4 convolution_add_fusion.5
  325.9 1.4 convolution_add_fusion.5
  327.3 1.4 convolution_add_fusion.5
  328.8 1.4 convolution_add_fusion.5
  331.8 1.4 convolution_add_fusion.5
  333.3 1.4 convolution_add_fusion.5
  (103 shorter events, 34.8 us)
Async XLA Ops:
  7.2 1.0 copy-start
  7.2 61.7 %copy-start.1 = (bf16[4,128,128]{2,1,0:T(8,128)(2,1)S(1)}, bf16[4,128,128]{2,1,0:T(8,128)(2,1)}, u32[]{:S(2)}) copy-start(bf16[4,128,128]{2,1,0:T(8,128)(2,1)} %param.16) | copy-start | bytes 393220
  7.2 61.7 %copy-start.5 = (f32[4,128]{1,0:T(4,128)S(1)}, f32[4,128]{1,0:T(4,128)}, u32[]{:S(2)}) copy-start(f32[4,128]{1,0:T(4,128)} %param.20) | copy-start | bytes 6148
  7.2 57.7 %copy-start.4 = (bf16[4,128,128]{2,1,0:T(8,128)(2,1)S(1)}, bf16[4,128,128]{2,1,0:T(8,128)(2,1)}, u32[]{:S(2)}) copy-start(bf16[4,128,128]{2,1,0:T(8,128)(2,1)} %param.17) | copy-start | bytes 393220
  7.2 59.3 %copy-start.6 = (f32[4,4,128]{2,1,0:T(4,128)S(1)}, f32[4,4,128]{2,1,0:T(4,128)}, u32[]{:S(2)}) copy-start(f32[4,4,128]{2,1,0:T(4,128)} %param.21) | copy-start | bytes 24580
  7.2 114.8 %all-gather.15.cloned.1.call-start = ((), (), s32[]{:S(2)}) async-start(), calls=%async_computation.3 | async-start | bytes 8650752 | tf_op jit(solution)/shard_map/all_gather | solution.py:22
  62.8 119.4 %all-gather.13.cloned.1.call-start = ((), (), s32[]{:S(2)}) async-start(), calls=%async_computation.2 | async-start | bytes 8650752 | tf_op jit(solution)/shard_map/all_gather | solution.py:22
  63.2 0.9 copy-start.2
  64.1 178.8 %all-gather.9.cloned.1.call-start = ((), (), s32[]{:S(2)}) async-start(), calls=%async_computation | async-start | bytes 8650752 | tf_op jit(solution)/shard_map/all_gather | solution.py:22
  64.8 238.6 %all-gather.11.cloned.1.call-start = ((), (), s32[]{:S(2)}) async-start(), calls=%async_computation.1 | async-start | bytes 8650752 | tf_op jit(solution)/shard_map/all_gather | solution.py:22
  64.9 3.2 collective-permute-start
  182.2 167.9 %copy-start.3 = (bf16[4,128,128]{2,1,0:T(8,128)(2,1)S(1)}, bf16[4,128,128]{2,1,0:T(8,128)(2,1)}, u32[]{:S(2)}) copy-start(bf16[4,128,128]{2,1,0:T(8,128)(2,1)} %param.18) | copy-start | bytes 393220
  183.1 168.9 %collective-permute-start.1 = (f32[4,3,128]{2,1,0:T(4,128)S(1)}, f32[4,3,128]{2,1,0:T(4,128)S(1)}, u32[]{:S(2)}, u32[]{:S(2)}) collective-permute-start(f32[4,3,128]{2,1,0:T(4,128)S(1)} %slice.73), channel_id=1, source_target_pairs={{8,0},{16,8},{24,16},{32,24},{40,32},{48,40},{56,48},{64,56},{72,6... | collective-permute-start | bytes 18440 | tf_op jit(solution)/shard_map/ppermute | solution.py:15
Sparse Core Ops, SparseCore 0:
  62.9 59.0 all-gather.14
  124.5 57.5 all-gather.12
  185.3 57.5 all-gather.8
  245.9 57.5 all-gather.10
where the time goes:
time: 360 us; the launch traced here: 359 us
  waiting for transfers between devices  231 us (64%)
  matrix products  63.4 us (18%)
  other arithmetic  42.5 us (12%)
  between operations  14.1 us (4%)
  starting transfers between devices  5.09 us (1%)
    all_gather x4, waiting for transfers between devices, prefix(): gathered = jax.tree.map(lambda a: lax.all_gather(a, axis), part)  228 us
    dot_general x33, matrix products, apply_left(): return jnp.einsum('hij,hjk->hik', matrix, other, precision=highest)  45 us
    another operation x3, other arithmetic, triangular(): jax.scipy.linalg.solve_triangular(system, right, trans=transpose_flag, lo...  39.4 us
  transfers between devices with their start and end apart: 6, of which 5 were waited for; matrix products, arithmetic and copies ran while one was open for 14% of the time, Pallas kernels for 0%

commit v1 on v0

v1 whole, which is shorter than its diff:
```python
import jax
import jax.numpy as jnp
from jax import lax
from jax.experimental import pallas as pl
from jax.experimental.pallas import tpu as pltpu
from jax.sharding import PartitionSpec as P

MESH = pl.DeviceIdType.MESH
F32 = jnp.float32
BF16 = jnp.bfloat16
HEADS = 4
N = 128
SIDE = 4
RING = 32


def split(a):
    high = a.astype(BF16)
    return high, (a - high.astype(F32)).astype(BF16)


def left(a):
    return jnp.concatenate(split(a), axis=1)


def right(*arrays):
    row = jnp.concatenate([part for a in arrays for part in split(a)], axis=1)
    return jnp.concatenate([row, row], axis=0)


def right_t(a):
    high, low = split(a)
    return jnp.concatenate(
        [jnp.concatenate([high, high], axis=1), jnp.concatenate([low, low], axis=1)], axis=0
    )


def halves(wide):
    return [
        wide[:, 2 * N * i : 2 * N * i + N] + wide[:, 2 * N * i + N : 2 * N * (i + 1)]
        for i in range(wide.shape[1] // (2 * N))
    ]


def mm(a, *bs):
    out = halves(jnp.dot(left(a), right(*bs), preferred_element_type=F32))
    return out[0] if len(bs) == 1 else out


def mm_t(a, b):
    return halves(
        lax.dot_general(
            left(a), right_t(b), (((1,), (1,)), ((), ())), preferred_element_type=F32
        )
    )[0]


def mm_exact(a, b):
    return jnp.dot(left(a), jnp.concatenate([b, b], axis=0), preferred_element_type=F32)


def kernel(
    q_ref, k_ref, v_ref, o_ref, g_ref, beta_ref, w_ref, qg_ref, ig_ref,
    tail, halo_v, padded, dsig, loc, pair, chip, row, tot, above, pref, start, sends, back, states,
    xk, pl_mix, wt, lg, kgc, e0, e1, pg_first, pg_next, pg_pad,
    tail_s, tail_r, pair_s, pair_r, row_s, row_r, up_s, up_r, back_s, back_r, fwd_s, fwd_r, pg_s, pg_r,
):
    me = lax.axis_index("ctx")
    head = lax.axis_index("head")
    c = lax.rem(me, 2)
    x = lax.rem(me // 2, SIDE)
    y = me // (2 * SIDE)

    def at(yy, xx, cc):
        return ((yy * SIDE + xx) * 2 + cc, head)

    def place(v):
        return v * (2 * c - 1) + (SIDE - 1) * (1 - c)

    p, r = place(x), place(y)
    partner = at(y, x, 1 - c)
    following = (lax.rem(me + 1, RING), head)
    preceding = (lax.rem(me + RING - 1, RING), head)
    other_near = (lax.rem(me + 2 * c - 1 + RING, RING), head)

    barrier = pltpu.get_barrier_semaphore()
    greeted = [partner, other_near]
    greeted += [at(y, lax.rem(x + d, SIDE), c) for d in range(1, SIDE)]
    greeted += [at(lax.rem(y + d, SIDE), x, c) for d in range(1, SIDE)]
    for device in greeted:
        pl.semaphore_signal(barrier, inc=1, device_id=device, device_id_type=MESH)

    def remote(src, dst, send, recv, device):
        return pltpu.make_async_remote_copy(
            src_ref=src, dst_ref=dst, send_sem=send, recv_sem=recv,
            device_id=device, device_id_type=MESH,
        )

    tail[...] = v_ref[:, N - 16 :, :]
    pl.semaphore_wait(barrier, len(greeted))
    tail_copy = remote(tail, halo_v, tail_s, tail_r, following)
    tail_copy.start()

    t_id = lax.broadcasted_iota(jnp.int32, (N, N), 0)
    s_id = lax.broadcasted_iota(jnp.int32, (N, N), 1)
    lower_ones = jnp.where(t_id >= s_id, 1.0, 0.0).astype(BF16)
    eye = jnp.where(t_id == s_id, 1.0, 0.0).astype(F32)

    def block_mask(small, large):
        return (t_id // large == s_id // large) & (t_id // small > s_id // small)

    heads = range(HEADS)
    system, kd_all, ket_all, ke_all, kdt_all, rhs_all, qto_all, keep_all = [[] for _ in range(8)]
    for h in heads:
        q = q_ref[h].astype(F32)
        q = q * lax.rsqrt(jnp.sum(q * q, axis=1, keepdims=True) + 1e-6)
        k = k_ref[h].astype(F32)
        k = k * lax.rsqrt(jnp.sum(k * k, axis=1, keepdims=True) + 1e-6)
        g = g_ref[h]
        g_high = g.astype(BF16)
        rest = g - g_high.astype(F32)
        g_mid = rest.astype(BF16)
        g_low = (rest - g_mid.astype(F32)).astype(BF16)
        sums = jnp.dot(
            lower_ones, jnp.concatenate([g_high, g_mid, g_low], axis=1), preferred_element_type=F32
        )
        ld = sums[:, :N] + (sums[:, N : 2 * N] + sums[:, 2 * N :])
        middle = ld[N // 2 - 1 : N // 2, :]
        last = ld[N - 1 :, :]
        since = jnp.exp(ld - middle)
        until = jnp.exp(middle - ld)
        full = since * jnp.exp(middle)
        to_end = until * jnp.exp(last - middle)
        e1[h] = since
        e0[h] = full
        beta_row = beta_ref[h : h + 1, :]
        beta_col = jnp.sum(eye * beta_row, axis=1, keepdims=True)
        k_until = k * until
        kgc[h] = k_until
        kd = k * full
        ke = k * to_end
        ket_all.append(ke.T * beta_row)
        ke_all.append(ke * beta_col)
        kd_all.append(kd)
        kdt_all.append(kd.T)
        mix = mm_t(k * since, k_until)
        system.append(jnp.where(t_id > s_id, mix * beta_row, 0.0))
        upper = jnp.where(s_id >= t_id, mm_t(k_until, q * since), 0.0)
        rhs_all.append(beta_col * mm_exact(upper, o_ref[h]))
        qto_all.append(mm_exact((q * full).T, o_ref[h]))
        keep_all.append(jnp.exp(last))

    inverse = [eye - jnp.where(block_mask(1, 2), system[h], 0.0) for h in heads]
    for small in (2, 8, 32):
        mask = block_mask(small, 4 * small)
        for h in heads:
            m = mm(inverse[h], jnp.where(mask, system[h], 0.0))
            squared, applied = mm(m, m, inverse[h])
            z = inverse[h] - applied
            inverse[h] = z + mm(squared, z)

    tail_copy.wait_recv()
    for h in heads:
        padded[h, 8:, :] = v_ref[h].astype(F32)
        edge = halo_v[h].astype(F32)[8:, :]
        padded[h, :8, :] = jnp.where(me > 0, edge, 0.0)
        pre = w_ref[0, h : h + 1, :] * padded[h, 8:, :]
        for j in range(1, 4):
            pre = pre + w_ref[j, h : h + 1, :] * padded[h, 8 - j : 8 - j + N, :]
        sig = jax.nn.sigmoid(pre)
        dsig[h] = sig * (1.0 + pre * (1.0 - sig))
        value = pre * sig
        keys_x, values_x = mm(inverse[h], kd_all[h], value)
        keys_xt = mm_t(kdt_all[h], inverse[h])
        fwd_t, fwd_f = mm(ket_all[h], keys_x, values_x)
        bwd_t, bwd_f = mm(keys_xt, ke_all[h], rhs_all[h])
        keep = eye * keep_all[h]
        loc[h, 0, 0] = keep - fwd_t
        loc[h, 0, 1] = fwd_f
        loc[h, 1, 0] = keep - bwd_t
        loc[h, 1, 1] = qto_all[h] - bwd_f
        xk[h] = keys_x
        remote(loc.at[h, c], pair.at[h], pair_s.at[h], pair_r.at[h], partner).start()
        out_values = lax.dot_general(
            jnp.concatenate([o_ref[h], o_ref[h]], axis=1), jnp.concatenate(split(values_x), axis=1),
            (((1,), (1,)), ((), ())), preferred_element_type=F32,
        )
        pl_mix[h] = jnp.where(t_id >= s_id, out_values, 0.0) * beta_ref[h : h + 1, :]
        wt[h], lg[h] = mm(inverse[h].T, ke_all[h], rhs_all[h])

    for h in heads:
        remote(loc.at[h, c], pair.at[h], pair_s.at[h], pair_r.at[h], partner).wait_recv()
        g_chip, f_chip = mm(loc[h, 1 - c, 0], pair[h, 0], pair[h, 1])
        chip[h, 0] = g_chip
        chip[h, 1] = f_chip + loc[h, 1 - c, 1]

        @pl.when(x != h)
        def _():
            remote(chip.at[h], row.at[p], row_s.at[h], row_r.at[p], at(y, h, c)).start()

        @pl.when(x == h)
        def _():
            row[p] = chip[h]

    for d in range(1, SIDE):
        source = lax.rem(x + d, SIDE)
        slot = place(source)
        remote(chip.at[0], row.at[slot], row_s.at[0], row_r.at[slot], at(y, source, c)).wait_recv()
    p2, o2 = mm(row[1, 0], row[0, 0], row[0, 1])
    o2 = o2 + row[1, 1]
    q2, r2 = mm(row[3, 0], row[2, 0], row[2, 1])
    r2 = r2 + row[3, 1]
    tg, tf = mm(q2, p2, o2)
    tot[0] = tg
    tot[1] = tf + r2

    def up(kind, target):
        return remote(
            tot.at[kind], above.at[r, kind], up_s.at[target, kind], up_r.at[r, kind],
            at(place(target), x, c),
        )

    for target in range(1, SIDE):
        @pl.when(r < target)
        def _():
            up(1, target).start()

        @pl.when((r < target) & (r > 0))
        def _():
            up(0, target).start()

    p3, o3 = mm(row[2, 0], p2, o2)
    pref[0, 0] = row[0, 0]
    pref[0, 1] = row[0, 1]
    pref[1, 0] = p2
    pref[1, 1] = o2
    pref[2, 0] = p3
    pref[2, 1] = o3 + row[2, 1]

    def got(source, kind):
        remote(
            tot.at[kind], above.at[source, kind], up_s.at[1, kind], up_r.at[source, kind], partner
        ).wait_recv()

    start[...] = jnp.zeros((N, N), F32)

    @pl.when(r >= 1)
    def _():
        got(0, 1)
        start[...] = above[0, 1]

    for source in (1, 2):
        @pl.when(r > source)
        def _():
            got(source, 0)
            got(source, 1)
            start[...] = mm(above[source, 0], start[...]) + above[source, 1]

    for target in range(SIDE):
        if target == 0:
            sends[0] = start[...]
        else:
            sends[target] = mm(pref[target - 1, 0], start[...]) + pref[target - 1, 1]
        to = place(target)

        @pl.when(to != x)
        def _():
            remote(
                sends.at[target], back.at[x], back_s.at[target], back_r.at[x], at(y, to, c)
            ).start()

        @pl.when(to == x)
        def _():
            back[x] = sends[target]

    for h in heads:
        @pl.when(x != h)
        def _():
            remote(sends.at[0], back.at[h], back_s.at[0], back_r.at[h], partner).wait_recv()

        remote(back.at[h], states.at[1 - c, h], fwd_s.at[h], fwd_r.at[h], partner).start()
        states[1 - c, h] = mm(pair[h, 0], back[h]) + pair[h, 1]

    for h in heads:
        remote(back.at[h], states.at[c, h], fwd_s.at[h], fwd_r.at[h], partner).wait_recv()
        pg = (lg[h] + mm(wt[h], states[1, h])) * dsig[h]
        pg_pad[h, :N, :] = pg
        pg_first[h] = pg[:8, :]
    pg_copy = remote(pg_first, pg_next, pg_s, pg_r, preceding)
    pg_copy.start()
    for h in heads:
        state = states[0, h]
        reach = lax.dot_general(
            jnp.concatenate([o_ref[h], o_ref[h]], axis=1),
            jnp.concatenate(split(state), axis=1),
            (((1,), (1,)), ((), ())), preferred_element_type=F32,
        )
        mixed = mm_t(reach, xk[h])
        weights = pl_mix[h] - jnp.where(t_id >= s_id, mixed, 0.0) * beta_ref[h : h + 1, :]
        qg_ref[h] = e1[h] * mm(weights, kgc[h]) + e0[h] * reach

    pg_copy.wait_recv()
    for h in heads:
        pg_pad[h, N:, :] = jnp.where(me < RING - 1, pg_next[h], 0.0)
        grad = w_ref[0, h : h + 1, :] * pg_pad[h, :N, :]
        for j in range(1, 4):
            grad = grad + w_ref[j, h : h + 1, :] * pg_pad[h, j : j + N, :]
        ig_ref[h] = grad

    tail_copy.wait_send()
    pg_copy.wait_send()
    for h in heads:
        remote(loc.at[h, c], pair.at[h], pair_s.at[h], pair_r.at[h], partner).wait_send()
        remote(back.at[h], states.at[1 - c, h], fwd_s.at[h], fwd_r.at[h], partner).wait_send()

        @pl.when(x != h)
        def _():
            remote(chip.at[h], row.at[p], row_s.at[h], row_r.at[p], at(y, h, c)).wait_send()

    for target in range(1, SIDE):
        @pl.when(r < target)
        def _():
            up(1, target).wait_send()

        @pl.when((r < target) & (r > 0))
        def _():
            up(0, target).wait_send()

    for target in range(SIDE):
        @pl.when(place(target) != x)
        def _():
            remote(
                sends.at[target], back.at[x], back_s.at[target], back_r.at[x], at(y, x, c)
            ).wait_send()


def local(queries, keys, values_in, out_grad, logged_keep_factor, beta, conv_weight):
    vmem = pl.BlockSpec(memory_space=pltpu.VMEM)
    sem = pltpu.SemaphoreType.DMA
    square = lambda *lead: pltpu.VMEM((*lead, N, N), F32)
    out = jax.ShapeDtypeStruct((HEADS, N, N), F32)
    return pl.pallas_call(
        kernel,
        out_shape=(out, out),
        in_specs=[vmem] * 7,
        out_specs=(vmem, vmem),
        scratch_shapes=[
            pltpu.VMEM((HEADS, 16, N), BF16),
            pltpu.VMEM((HEADS, 16, N), BF16),
            pltpu.VMEM((HEADS, N + 8, N), F32),
            square(HEADS),
            square(HEADS, 2, 2),
            square(HEADS, 2),
            square(HEADS, 2),
            square(SIDE, 2),
            square(2),
            square(SIDE - 1, 2),
            square(SIDE - 1, 2),
            square(),
            square(SIDE),
            square(HEADS),
            square(2, HEADS),
            square(HEADS),
            square(HEADS),
            square(HEADS),
            square(HEADS),
            square(HEADS),
            square(HEADS),
            square(HEADS),
            pltpu.VMEM((HEADS, 8, N), F32),
            pltpu.VMEM((HEADS, 8, N), F32),
            pltpu.VMEM((HEADS, N + 8, N), F32),
            sem, sem,
            sem((HEADS,)), sem((HEADS,)),
            sem((HEADS,)), sem((SIDE,)),
            sem((SIDE, 2)), sem((SIDE, 2)),
            sem((SIDE,)), sem((HEADS,)),
            sem((HEADS,)), sem((HEADS,)),
            sem, sem,
        ],
        compiler_params=pltpu.CompilerParams(
            collective_id=0, has_side_effects=True, vmem_limit_bytes=40 * 2**20
        ),
        name="delta_backward",
    )(queries, keys, values_in, out_grad, logged_keep_factor, beta, conv_weight)


def solution(mesh):
    in_specs = (
        P("head", "ctx", None),
        P("head", "ctx", None),
        P("head", "ctx", None),
        P("head", "ctx", None),
        P("head", "ctx", None),
        P("head", "ctx"),
        P(None, "head", None),
    )
    out_specs = (P("head", "ctx", None), P("head", "ctx", None))
    return jax.shard_map(local, mesh=mesh, in_specs=in_specs, out_specs=out_specs, check_vma=False)
```

time: 360 us -> 43.8 us (0.12)
  the two profiles are of different devices: /device:TPU:31 before, /device:TPU:1 now
where the time goes in v1:
time: 43.8 us; the launch traced here: 43.5 us
  Pallas kernels  35.5 us (81%)
  local copies, waits for them, and re-layouts  7.34 us (17%)
  between operations  0.66 us (2%)
    pallas_call x1, Pallas kernels, local(): pl.pallas_call(kernel, out_shape=(out, out), in_specs=[vmem] * 7, out_spe...  35.5 us
    unnamed x16, local copies, waits for them, and re-layouts  7.34 us

profile of v1, /device:TPU:1, one launch (start us, length us, event | category | flops | bytes accessed | tf_op | source)
XLA Modules:
  0.0 43.5 jit_solution(5092659547620731788)
XLA Ops:
  0.6 0.0 copy-start
  0.6 0.9 %copy-done = f32[4,128,128]{2,1,0:T(8,128)S(1)} copy-done((f32[4,128,128]{2,1,0:T(8,128)S(1)}, f32[4,128,128]{2,1,0:T(8,128)}, u32[]{:S(2)}) %copy-start) | copy-done | bytes 262168
  1.6 0.0 copy-start.1
  1.6 0.9 %copy-done.1 = bf16[4,128,128]{2,1,0:T(8,128)(2,1)S(1)} copy-done((bf16[4,128,128]{2,1,0:T(8,128)(2,1)S(1)}, bf16[4,128,128]{2,1,0:T(8,128)(2,1)}, u32[]{:S(2)}) %copy-start.1) | copy-done | bytes 131096
  2.5 0.0 copy-start.2
  2.5 0.9 %copy-done.2 = bf16[4,128,128]{2,1,0:T(8,128)(2,1)S(1)} copy-done((bf16[4,128,128]{2,1,0:T(8,128)(2,1)S(1)}, bf16[4,128,128]{2,1,0:T(8,128)(2,1)}, u32[]{:S(2)}) %copy-start.2) | copy-done | bytes 131096
  3.4 0.0 copy-start.3
  3.4 0.9 %copy-done.3 = bf16[4,128,128]{2,1,0:T(8,128)(2,1)S(1)} copy-done((bf16[4,128,128]{2,1,0:T(8,128)(2,1)S(1)}, bf16[4,128,128]{2,1,0:T(8,128)(2,1)}, u32[]{:S(2)}) %copy-start.3) | copy-done | bytes 131096
  4.3 0.0 copy-start.4
  4.3 0.9 %copy-done.4 = bf16[4,128,128]{2,1,0:T(8,128)(2,1)S(1)} copy-done((bf16[4,128,128]{2,1,0:T(8,128)(2,1)S(1)}, bf16[4,128,128]{2,1,0:T(8,128)(2,1)}, u32[]{:S(2)}) %copy-start.4) | copy-done | bytes 131096
  5.2 0.0 copy-start.5
  5.2 0.7 %copy-done.5 = f32[4,4,128]{2,1,0:T(4,128)S(1)} copy-done((f32[4,4,128]{2,1,0:T(4,128)S(1)}, f32[4,4,128]{2,1,0:T(4,128)}, u32[]{:S(2)}) %copy-start.5) | copy-done | bytes 8216
  5.9 0.0 copy-start.6
  5.9 0.7 %copy-done.6 = f32[4,128]{1,0:T(4,128)S(1)} copy-done((f32[4,128]{1,0:T(4,128)S(1)}, f32[4,128]{1,0:T(4,128)}, u32[]{:S(2)}) %copy-start.6) | copy-done | bytes 2072
  6.6 35.5 %delta_backward.1 = (f32[4,128,128]{2,1,0:T(8,128)S(1)}, f32[4,128,128]{2,1,0:T(8,128)S(1)}) custom-call(bf16[4,128,128]{2,1,0:T(8,128)(2,1)S(1)} %copy-done.1, bf16[4,128,128]{2,1,0:T(8,128)(2,1)S(1)} %copy-done.2, bf16[4,128,128]{2,1,0:T(8,128)(2,1)S(1)} %copy-done.3, bf16[4,128,128]{2,1,0:T(8,128)(2,1)S(1)} %copy-done.4, f32[4,128,128]{2,1,0:T(8,128)S(1)} %copy-done, ...), custom_call_target="tpu_custom_call" | custom-call | tf_op jit(solution)/shard_map/delta_backward/pallas_call | solution.py:342
  42.1 0.7 %copy.11 = f32[4,128,128]{2,1,0:T(8,128)} copy(f32[4,128,128]{2,1,0:T(8,128)S(1)} %get-tuple-element.4) | data formatting | bytes 524288
  42.8 0.7 %copy.12 = f32[4,128,128]{2,1,0:T(8,128)} copy(f32[4,128,128]{2,1,0:T(8,128)S(1)} %get-tuple-element.5) | data formatting | bytes 524288
Async XLA Ops:
  0.6 1.0 %copy-start = (f32[4,128,128]{2,1,0:T(8,128)S(1)}, f32[4,128,128]{2,1,0:T(8,128)}, u32[]{:S(2)}) copy-start(f32[4,128,128]{2,1,0:T(8,128)} %g_ref.1) | copy-start | bytes 786436
  1.6 0.9 %copy-start.1 = (bf16[4,128,128]{2,1,0:T(8,128)(2,1)S(1)}, bf16[4,128,128]{2,1,0:T(8,128)(2,1)}, u32[]{:S(2)}) copy-start(bf16[4,128,128]{2,1,0:T(8,128)(2,1)} %q_ref.1) | copy-start | bytes 393220
  2.5 0.9 %copy-start.2 = (bf16[4,128,128]{2,1,0:T(8,128)(2,1)S(1)}, bf16[4,128,128]{2,1,0:T(8,128)(2,1)}, u32[]{:S(2)}) copy-start(bf16[4,128,128]{2,1,0:T(8,128)(2,1)} %k_ref.1) | copy-start | bytes 393220
  3.4 0.9 %copy-start.3 = (bf16[4,128,128]{2,1,0:T(8,128)(2,1)S(1)}, bf16[4,128,128]{2,1,0:T(8,128)(2,1)}, u32[]{:S(2)}) copy-start(bf16[4,128,128]{2,1,0:T(8,128)(2,1)} %v_ref.1) | copy-start | bytes 393220
  4.3 0.9 %copy-start.4 = (bf16[4,128,128]{2,1,0:T(8,128)(2,1)S(1)}, bf16[4,128,128]{2,1,0:T(8,128)(2,1)}, u32[]{:S(2)}) copy-start(bf16[4,128,128]{2,1,0:T(8,128)(2,1)} %o_ref.1) | copy-start | bytes 393220
  5.2 0.7 %copy-start.5 = (f32[4,4,128]{2,1,0:T(4,128)S(1)}, f32[4,4,128]{2,1,0:T(4,128)}, u32[]{:S(2)}) copy-start(f32[4,4,128]{2,1,0:T(4,128)} %w_ref.1) | copy-start | bytes 24580
  5.9 0.7 %copy-start.6 = (f32[4,128]{1,0:T(4,128)S(1)}, f32[4,128]{1,0:T(4,128)}, u32[]{:S(2)}) copy-start(f32[4,128]{1,0:T(4,128)} %beta_ref.1) | copy-start | bytes 6148

commit v2 on v1

--- a/solution.py
+++ b/solution.py
@@ -60,9 +60,11 @@
 
 
 def kernel(
-    q_ref, k_ref, v_ref, o_ref, g_ref, beta_ref, w_ref, qg_ref, ig_ref,
-    tail, halo_v, padded, dsig, loc, pair, chip, row, tot, above, pref, start, sends, back, states,
-    xk, pl_mix, wt, lg, kgc, e0, e1, pg_first, pg_next, pg_pad,
+    q_hbm, k_hbm, v_hbm, o_hbm, g_hbm, beta_hbm, w_hbm, qg_ref, ig_ref,
+    q_ref, k_ref, v_ref, o_ref, g_ref, beta_ref, w_ref,
+    halo_v, padded, dsig, loc, pair, chip, row, tot, above, pref, start, sends, back, other,
+    inv, rhs, ke, xv, xk, pl_mix, wt, lg, kgc, e0, e1, pg_first, pg_next, pg_pad,
+    load_s,
     tail_s, tail_r, pair_s, pair_r, row_s, row_r, up_s, up_r, back_s, back_r, fwd_s, fwd_r, pg_s, pg_r,
 ):
     me = lax.axis_index("ctx")
@@ -83,6 +85,18 @@
     preceding = (lax.rem(me + RING - 1, RING), head)
     other_near = (lax.rem(me + 2 * c - 1 + RING, RING), head)
 
+    loads = [
+        pltpu.make_async_copy(src, dst, load_s.at[i])
+        for i, (src, dst) in enumerate(
+            (
+                (k_hbm, k_ref), (g_hbm, g_ref), (beta_hbm, beta_ref), (q_hbm, q_ref),
+                (o_hbm, o_ref), (v_hbm, v_ref), (w_hbm, w_ref),
+            )
+        )
+    ]
+    for load in loads:
+        load.start()
+
     barrier = pltpu.get_barrier_semaphore()
     greeted = [partner, other_near]
     greeted += [at(y, lax.rem(x + d, SIDE), c) for d in range(1, SIDE)]
@@ -96,10 +110,7 @@
             device_id=device, device_id_type=MESH,
         )
 
-    tail[...] = v_ref[:, N - 16 :, :]
-    pl.semaphore_wait(barrier, len(greeted))
-    tail_copy = remote(tail, halo_v, tail_s, tail_r, following)
-    tail_copy.start()
+    pending = []
 
     t_id = lax.broadcasted_iota(jnp.int32, (N, N), 0)
     s_id = lax.broadcasted_iota(jnp.int32, (N, N), 1)
@@ -110,10 +121,11 @@
         return (t_id // large == s_id // large) & (t_id // small > s_id // small)
 
     heads = range(HEADS)
-    system, kd_all, ket_all, ke_all, kdt_all, rhs_all, qto_all, keep_all = [[] for _ in range(8)]
-    for h in heads:
-        q = q_ref[h].astype(F32)
-        q = q * lax.rsqrt(jnp.sum(q * q, axis=1, keepdims=True) + 1e-6)
+    system, kd_all, ket_all, kdt_all, qto_all, keep_all, beta_col_all, qn_all = [[] for _ in range(8)]
+    for load in loads[:3]:
+        load.wait()
+    since_all, full_all = [], []
+    for h in heads:
         k = k_ref[h].astype(F32)
         k = k * lax.rsqrt(jnp.sum(k * k, axis=1, keepdims=True) + 1e-6)
         g = g_ref[h]
@@ -134,21 +146,23 @@
         e1[h] = since
         e0[h] = full
         beta_row = beta_ref[h : h + 1, :]
-        beta_col = jnp.sum(eye * beta_row, axis=1, keepdims=True)
         k_until = k * until
         kgc[h] = k_until
-        kd = k * full
-        ke = k * to_end
-        ket_all.append(ke.T * beta_row)
-        ke_all.append(ke * beta_col)
-        kd_all.append(kd)
-        kdt_all.append(kd.T)
         mix = mm_t(k * since, k_until)
         system.append(jnp.where(t_id > s_id, mix * beta_row, 0.0))
-        upper = jnp.where(s_id >= t_id, mm_t(k_until, q * since), 0.0)
-        rhs_all.append(beta_col * mm_exact(upper, o_ref[h]))
-        qto_all.append(mm_exact((q * full).T, o_ref[h]))
+        beta_col_all.append(jnp.sum(eye * beta_row, axis=1, keepdims=True))
+        kd_all.append(k * full)
+        qn_all.append(k * to_end)
+        since_all.append(since)
+        full_all.append(full)
         keep_all.append(jnp.exp(last))
+
+    pl.semaphore_wait(barrier, len(greeted))
+    tail_copy = remote(v_hbm.at[:, N - 16 :, :], halo_v, tail_s, tail_r, following)
+    tail_copy.start()
+    pending.append(tail_copy.wait_send)
+    for load in loads[3:]:
+        load.wait()
 
     inverse = [eye - jnp.where(block_mask(1, 2), system[h], 0.0) for h in heads]
     for small in (2, 8, 32):
@@ -158,8 +172,20 @@
             squared, applied = mm(m, m, inverse[h])
             z = inverse[h] - applied
             inverse[h] = z + mm(squared, z)
+    for h in heads:
+        inv[h] = inverse[h]
+        k_end = qn_all[h]
+        ket_all.append(k_end.T * beta_ref[h : h + 1, :])
+        ke[h] = k_end * beta_col_all[h]
+        kdt_all.append(kd_all[h].T)
+        q = q_ref[h].astype(F32)
+        q = q * lax.rsqrt(jnp.sum(q * q, axis=1, keepdims=True) + 1e-6)
+        upper = jnp.where(s_id >= t_id, mm_t(kgc[h], q * since_all[h]), 0.0)
+        rhs[h] = beta_col_all[h] * mm_exact(upper, o_ref[h])
+        qto_all.append(mm_exact((q * full_all[h]).T, o_ref[h]))
 
     tail_copy.wait_recv()
+    pair_copies = []
     for h in heads:
         padded[h, 8:, :] = v_ref[h].astype(F32)
         edge = halo_v[h].astype(F32)[8:, :]
@@ -173,34 +199,47 @@
         keys_x, values_x = mm(inverse[h], kd_all[h], value)
         keys_xt = mm_t(kdt_all[h], inverse[h])
         fwd_t, fwd_f = mm(ket_all[h], keys_x, values_x)
-        bwd_t, bwd_f = mm(keys_xt, ke_all[h], rhs_all[h])
+        bwd_t, bwd_f = mm(keys_xt, ke[h], rhs[h])
         keep = eye * keep_all[h]
         loc[h, 0, 0] = keep - fwd_t
         loc[h, 0, 1] = fwd_f
         loc[h, 1, 0] = keep - bwd_t
         loc[h, 1, 1] = qto_all[h] - bwd_f
         xk[h] = keys_x
-        remote(loc.at[h, c], pair.at[h], pair_s.at[h], pair_r.at[h], partner).start()
-        out_values = lax.dot_general(
-            jnp.concatenate([o_ref[h], o_ref[h]], axis=1), jnp.concatenate(split(values_x), axis=1),
-            (((1,), (1,)), ((), ())), preferred_element_type=F32,
-        )
-        pl_mix[h] = jnp.where(t_id >= s_id, out_values, 0.0) * beta_ref[h : h + 1, :]
-        wt[h], lg[h] = mm(inverse[h].T, ke_all[h], rhs_all[h])
-
-    for h in heads:
+        xv[h] = values_x
+        copy = remote(loc.at[h, c], pair.at[h], pair_s.at[h], pair_r.at[h], partner)
+        copy.start()
+        pair_copies.append(copy)
+        pending.append(copy.wait_send)
+
+    for d in (2, 1, 3, 0):
+        h = lax.rem(x + d, SIDE)
         remote(loc.at[h, c], pair.at[h], pair_s.at[h], pair_r.at[h], partner).wait_recv()
         g_chip, f_chip = mm(loc[h, 1 - c, 0], pair[h, 0], pair[h, 1])
-        chip[h, 0] = g_chip
-        chip[h, 1] = f_chip + loc[h, 1 - c, 1]
-
-        @pl.when(x != h)
-        def _():
-            remote(chip.at[h], row.at[p], row_s.at[h], row_r.at[p], at(y, h, c)).start()
-
-        @pl.when(x == h)
-        def _():
-            row[p] = chip[h]
+        if d == 0:
+            row[p, 0] = g_chip
+            row[p, 1] = f_chip + loc[h, 1 - c, 1]
+        else:
+            chip[d, 0] = g_chip
+            chip[d, 1] = f_chip + loc[h, 1 - c, 1]
+            copy = remote(chip.at[d], row.at[p], row_s.at[d], row_r.at[p], at(y, h, c))
+            copy.start()
+            pending.append(copy.wait_send)
+
+    for h in heads:
+        out_values = lax.dot_general(
+            jnp.concatenate([o_ref[h], o_ref[h]], axis=1), jnp.concatenate(split(xv[h]), axis=1),
+            (((1,), (1,)), ((), ())), preferred_element_type=F32,
+        )
+        pl_mix[h] = jnp.where(t_id >= s_id, out_values, 0.0) * beta_ref[h : h + 1, :]
+        wt[h], lg[h] = mm(inv[h].T, ke[h], rhs[h])
+
+    @pl.when(c == 0)
+    def _():
+        for h in heads:
+            through, extra = mm(wt[h], pair[h, 0], pair[h, 1])
+            wt[h] = through
+            lg[h] = lg[h] + extra
 
     for d in range(1, SIDE):
         source = lax.rem(x + d, SIDE)
@@ -229,6 +268,17 @@
         def _():
             up(0, target).start()
 
+        def drain(target=target):
+            @pl.when(r < target)
+            def _():
+                up(1, target).wait_send()
+
+            @pl.when((r < target) & (r > 0))
+            def _():
+                up(0, target).wait_send()
+
+        pending.append(drain)
+
     p3, o3 = mm(row[2, 0], p2, o2)
     pref[0, 0] = row[0, 0]
     pref[0, 1] = row[0, 1]
@@ -262,34 +312,46 @@
         else:
             sends[target] = mm(pref[target - 1, 0], start[...]) + pref[target - 1, 1]
         to = place(target)
+        copy = remote(
+            sends.at[target], back.at[x], back_s.at[target], back_r.at[x], at(y, to, c)
+        )
 
         @pl.when(to != x)
         def _():
-            remote(
-                sends.at[target], back.at[x], back_s.at[target], back_r.at[x], at(y, to, c)
-            ).start()
+            copy.start()
 
         @pl.when(to == x)
         def _():
             back[x] = sends[target]
 
-    for h in heads:
-        @pl.when(x != h)
-        def _():
-            remote(sends.at[0], back.at[h], back_s.at[0], back_r.at[h], partner).wait_recv()
-
-        remote(back.at[h], states.at[1 - c, h], fwd_s.at[h], fwd_r.at[h], partner).start()
-        states[1 - c, h] = mm(pair[h, 0], back[h]) + pair[h, 1]
-
-    for h in heads:
-        remote(back.at[h], states.at[c, h], fwd_s.at[h], fwd_r.at[h], partner).wait_recv()
-        pg = (lg[h] + mm(wt[h], states[1, h])) * dsig[h]
-        pg_pad[h, :N, :] = pg
-        pg_first[h] = pg[:8, :]
-    pg_copy = remote(pg_first, pg_next, pg_s, pg_r, preceding)
-    pg_copy.start()
-    for h in heads:
-        state = states[0, h]
+        def drain(to=to, copy=copy):
+            @pl.when(to != x)
+            def _():
+                copy.wait_send()
+
+        pending.append(drain)
+
+    forwards = [
+        remote(back.at[h], other.at[h], fwd_s.at[h], fwd_r.at[h], partner) for h in heads
+    ]
+
+    def hand_on():
+        for h in heads:
+            @pl.when(x != h)
+            def _():
+                remote(sends.at[0], back.at[h], back_s.at[0], back_r.at[h], partner).wait_recv()
+
+            forwards[h].start()
+
+    def gradients(carries):
+        for h in heads:
+            if carries is other:
+                forwards[h].wait_recv()
+            pg = (lg[h] + mm(wt[h], carries[h])) * dsig[h]
+            pg_pad[h, :N, :] = pg
+            pg_first[h] = pg[:8, :]
+
+    def queries(h, state):
         reach = lax.dot_general(
             jnp.concatenate([o_ref[h], o_ref[h]], axis=1),
             jnp.concatenate(split(state), axis=1),
@@ -299,59 +361,81 @@
         weights = pl_mix[h] - jnp.where(t_id >= s_id, mixed, 0.0) * beta_ref[h : h + 1, :]
         qg_ref[h] = e1[h] * mm(weights, kgc[h]) + e0[h] * reach
 
+    pg_copy = remote(pg_first, pg_next, pg_s, pg_r, preceding)
+
+    @pl.when(c == 0)
+    def _():
+        hand_on()
+        gradients(back)
+        pg_copy.start()
+        for h in heads:
+            forwards[h].wait_recv()
+            queries(h, other[h])
+
+    @pl.when(c == 1)
+    def _():
+        hand_on()
+        for h in heads:
+            queries(h, mm(pair[h, 0], back[h]) + pair[h, 1])
+        gradients(other)
+        pg_copy.start()
+
+    pending += [pg_copy.wait_send] + [copy.wait_send for copy in forwards]
+    body = N - 8
+
+    def mixed_rows(h, first, count):
+        grad = w_ref[0, h : h + 1, :] * pg_pad[h, first : first + count, :]
+        for j in range(1, 4):
+            grad = grad + w_ref[j, h : h + 1, :] * pg_pad[h, first + j : first + j + count, :]
+        ig_ref[h, first : first + count, :] = grad
+
+    for h in heads:
+        mixed_rows(h, 0, body)
     pg_copy.wait_recv()
     for h in heads:
         pg_pad[h, N:, :] = jnp.where(me < RING - 1, pg_next[h], 0.0)
-        grad = w_ref[0, h : h + 1, :] * pg_pad[h, :N, :]
-        for j in range(1, 4):
-            grad = grad + w_ref[j, h : h + 1, :] * pg_pad[h, j : j + N, :]
-        ig_ref[h] = grad
-
-    tail_copy.wait_send()
-    pg_copy.wait_send()
-    for h in heads:
-        remote(loc.at[h, c], pair.at[h], pair_s.at[h], pair_r.at[h], partner).wait_send()
-        remote(back.at[h], states.at[1 - c, h], fwd_s.at[h], fwd_r.at[h], partner).wait_send()
-
-        @pl.when(x != h)
-        def _():
-            remote(chip.at[h], row.at[p], row_s.at[h], row_r.at[p], at(y, h, c)).wait_send()
-
-    for target in range(1, SIDE):
-        @pl.when(r < target)
-        def _():
-            up(1, target).wait_send()
-
-        @pl.when((r < target) & (r > 0))
-        def _():
-            up(0, target).wait_send()
-
-    for target in range(SIDE):
-        @pl.when(place(target) != x)
-        def _():
-            remote(
-                sends.at[target], back.at[x], back_s.at[target], back_r.at[x], at(y, x, c)
-            ).wait_send()
+        mixed_rows(h, body, 8)
+    for wait in pending:
+        wait()
+
+
+def deliver(qg_from, ig_from, qg_to, ig_to, sems):
+    copies = [
+        pltpu.make_async_copy(src.at[h], dst.at[h], sems.at[i, h])
+        for i, (src, dst) in enumerate(((qg_from, qg_to), (ig_from, ig_to)))
+        for h in range(HEADS)
+    ]
+    for copy in copies:
+        copy.start()
+    for copy in copies:
+        copy.wait()
 
 
 def local(queries, keys, values_in, out_grad, logged_keep_factor, beta, conv_weight):
     vmem = pl.BlockSpec(memory_space=pltpu.VMEM)
+    hbm = pl.BlockSpec(memory_space=pltpu.HBM)
     sem = pltpu.SemaphoreType.DMA
     square = lambda *lead: pltpu.VMEM((*lead, N, N), F32)
     out = jax.ShapeDtypeStruct((HEADS, N, N), F32)
-    return pl.pallas_call(
+    grads = pl.pallas_call(
         kernel,
-        out_shape=(out, out),
-        in_specs=[vmem] * 7,
+        out_shape=(pltpu.VMEM((HEADS, N, N), F32),) * 2,
+        in_specs=[hbm] * 7,
         out_specs=(vmem, vmem),
         scratch_shapes=[
-            pltpu.VMEM((HEADS, 16, N), BF16),
+            pltpu.VMEM((HEADS, N, N), BF16),
+            pltpu.VMEM((HEADS, N, N), BF16),
+            pltpu.VMEM((HEADS, N, N), BF16),
+            pltpu.VMEM((HEADS, N, N), BF16),
+            square(HEADS),
+            pltpu.VMEM((HEADS, N), F32),
+            pltpu.VMEM((4, HEADS, N), F32),
             pltpu.VMEM((HEADS, 16, N), BF16),
             pltpu.VMEM((HEADS, N + 8, N), F32),
             square(HEADS),
             square(HEADS, 2, 2),
             square(HEADS, 2),
-            square(HEADS, 2),
+            square(SIDE, 2),
             square(SIDE, 2),
             square(2),
             square(SIDE - 1, 2),
@@ -359,7 +443,11 @@
             square(),
             square(SIDE),
             square(HEADS),
-            square(2, HEADS),
+            square(HEADS),
+            square(HEADS),
+            square(HEADS),
+            square(HEADS),
+            square(HEADS),
             square(HEADS),
             square(HEADS),
             square(HEADS),
@@ -370,19 +458,29 @@
             pltpu.VMEM((HEADS, 8, N), F32),
             pltpu.VMEM((HEADS, 8, N), F32),
             pltpu.VMEM((HEADS, N + 8, N), F32),
+            sem((7,)),
             sem, sem,
             sem((HEADS,)), sem((HEADS,)),
-            sem((HEADS,)), sem((SIDE,)),
+            sem((SIDE,)), sem((SIDE,)),
             sem((SIDE, 2)), sem((SIDE, 2)),
             sem((SIDE,)), sem((HEADS,)),
             sem((HEADS,)), sem((HEADS,)),
             sem, sem,
         ],
         compiler_params=pltpu.CompilerParams(
-            collective_id=0, has_side_effects=True, vmem_limit_bytes=40 * 2**20
+            collective_id=0, has_side_effects=True, vmem_limit_bytes=56 * 2**20
         ),
         name="delta_backward",
     )(queries, keys, values_in, out_grad, logged_keep_factor, beta, conv_weight)
+    return pl.pallas_call(
+        deliver,
+        out_shape=(out, out),
+        in_specs=[vmem] * 2,
+        out_specs=(hbm, hbm),
+        scratch_shapes=[sem((2, HEADS))],
+        compiler_params=pltpu.CompilerParams(vmem_limit_bytes=8 * 2**20),
+        name="deliver",
+    )(*grads)
 
 
 def solution(mesh):

time: 43.8 us -> 35.2 us (0.80)
  local copies, waits for them, and re-layouts: 7.34 us -> 0 us
  Pallas kernels: 35.5 us -> 34.5 us
    unnamed x16 -> x0, local copies, waits for them, and re-layouts: 7.34 us -> none
    pallas_call x1 -> x2, Pallas kernels: 35.5 us -> 34.5 us  [the longest x1 33.6 us: local(): pl.pallas_call(kernel, out_shape=(pltpu.VMEM((HEADS, N, N), F32),) * 2, i...]
where the time goes in v2:
time: 35.2 us; the launch traced here: 35.1 us
  Pallas kernels  34.5 us (98%)
  between operations  0.64 us (2%)
    pallas_call x1, Pallas kernels, local(): pl.pallas_call(kernel, out_shape=(pltpu.VMEM((HEADS, N, N), F32),) * 2, i...  33.6 us
    pallas_call x1, Pallas kernels, local(): pl.pallas_call(deliver, out_shape=(out, out), in_specs=[vmem] * 2, out_sp...  0.85 us

profile of v2, /device:TPU:1, one launch (start us, length us, event | category | flops | bytes accessed | tf_op | source)
XLA Modules:
  0.0 35.1 jit_solution(16567665694717679035)
XLA Ops:
  0.6 33.6 %delta_backward.1 = (f32[4,128,128]{2,1,0:T(8,128)S(1)}, f32[4,128,128]{2,1,0:T(8,128)S(1)}) custom-call(bf16[4,128,128]{2,1,0:T(8,128)(2,1)} %q_hbm.1, bf16[4,128,128]{2,1,0:T(8,128)(2,1)} %k_hbm.1, bf16[4,128,128]{2,1,0:T(8,128)(2,1)} %v_hbm.1, bf16[4,128,128]{2,1,0:T(8,128)(2,1)} %o_hbm.1, f32[4,128,128]{2,1,0:T(8,128)} %g_hbm.1, f32[4,128]{1,0:T(4,128)} %beta_hbm.1, ...), custom_call_target="tpu_custom_call" | custom-call | tf_op jit(solution)/shard_map/delta_backward/pallas_call | solution.py:420
  34.3 0.9 %deliver.1 = (f32[4,128,128]{2,1,0:T(8,128)}, f32[4,128,128]{2,1,0:T(8,128)}) custom-call(f32[4,128,128]{2,1,0:T(8,128)S(1)} %get-tuple-element.4.qg_from, f32[4,128,128]{2,1,0:T(8,128)S(1)} %get-tuple-element.5.ig_from), custom_call_target="tpu_custom_call" | custom-call | tf_op jit(solution)/shard_map/deliver/pallas_call | solution.py:475

commit v3 on v2

--- a/solution.py
+++ b/solution.py
@@ -63,9 +63,10 @@
     q_hbm, k_hbm, v_hbm, o_hbm, g_hbm, beta_hbm, w_hbm, qg_ref, ig_ref,
     q_ref, k_ref, v_ref, o_ref, g_ref, beta_ref, w_ref,
     halo_v, padded, dsig, loc, pair, chip, row, tot, above, pref, start, sends, back, other,
-    inv, rhs, ke, xv, xk, pl_mix, wt, lg, kgc, e0, e1, pg_first, pg_next, pg_pad,
+    inv, rhs, ke, xv, xk, pl_mix, wt, lg, kgc, e0, e1, edge_out, edge_in, edge_pre, edges, near, pg_next, pg_pad,
     load_s,
-    tail_s, tail_r, pair_s, pair_r, row_s, row_r, up_s, up_r, back_s, back_r, fwd_s, fwd_r, pg_s, pg_r,
+    tail_s, tail_r, pair_s, pair_r, row_s, row_r, up_s, up_r, back_s, back_r, fwd_s, fwd_r, pg_s, pg_r, edge_s, edge_r,
+    near_s, near_r,
 ):
     me = lax.axis_index("ctx")
     head = lax.axis_index("head")
@@ -82,7 +83,11 @@
     p, r = place(x), place(y)
     partner = at(y, x, 1 - c)
     following = (lax.rem(me + 1, RING), head)
-    preceding = (lax.rem(me + RING - 1, RING), head)
+
+    def before(chip_x):
+        return lax.rem((y * SIDE + chip_x) * 2 + RING - 1, RING)
+
+    next_row = lax.rem(me + 1, RING) // (2 * SIDE)
     other_near = (lax.rem(me + 2 * c - 1 + RING, RING), head)
 
     loads = [
@@ -101,6 +106,9 @@
     greeted = [partner, other_near]
     greeted += [at(y, lax.rem(x + d, SIDE), c) for d in range(1, SIDE)]
     greeted += [at(lax.rem(y + d, SIDE), x, c) for d in range(1, SIDE)]
+    greeted += [
+        (jnp.where(c == 0, before(i), (next_row * SIDE + i) * 2), head) for i in range(SIDE)
+    ]
     for device in greeted:
         pl.semaphore_signal(barrier, inc=1, device_id=device, device_id_type=MESH)
 
@@ -241,6 +249,29 @@
             wt[h] = through
             lg[h] = lg[h] + extra
 
+    for h in heads:
+        edge_out[h, 0] = wt[h, :8, :]
+        edge_out[h, 1] = lg[h, :8, :]
+        edge_out[h, 2] = dsig[h, :8, :]
+    near_copy = remote(edge_out, near, near_s, near_r, partner)
+    edge_copies = [
+        remote(
+            edge_out.at[lax.rem(x + d, SIDE)], edge_in.at[p], edge_s.at[d], edge_r.at[p],
+            at(y, lax.rem(x + d, SIDE), c),
+        )
+        for d in range(1, SIDE)
+    ]
+
+    @pl.when(c == 1)
+    def _():
+        near_copy.start()
+
+    @pl.when(c == 0)
+    def _():
+        for copy in edge_copies:
+            copy.start()
+        edge_in[p] = edge_out[x]
+
     for d in range(1, SIDE):
         source = lax.rem(x + d, SIDE)
         slot = place(source)
@@ -287,6 +318,20 @@
     pref[2, 0] = p3
     pref[2, 1] = o3 + row[2, 1]
 
+    @pl.when(c == 0)
+    def _():
+        for d in range(1, SIDE):
+            slot = place(lax.rem(x + d, SIDE))
+            remote(
+                edge_out.at[0], edge_in.at[slot], edge_s.at[1], edge_r.at[slot], partner
+            ).wait_recv()
+        edge_pre[0, :8, :] = edge_in[0, 0]
+        edge_pre[1, :8, :] = edge_in[0, 1]
+        for i in range(1, SIDE):
+            through, extra = mm(edge_in[i, 0], pref[i - 1, 0], pref[i - 1, 1])
+            edge_pre[0, 8 * i : 8 * i + 8, :] = through
+            edge_pre[1, 8 * i : 8 * i + 8, :] = extra + edge_in[i, 1]
+
     def got(source, kind):
         remote(
             tot.at[kind], above.at[source, kind], up_s.at[1, kind], up_r.at[source, kind], partner
@@ -331,6 +376,21 @@
 
         pending.append(drain)
 
+    edge_sends = [
+        remote(edges.at[i], pg_next.at[x], pg_s.at[i], pg_r.at[x], (before(place(i)), head))
+        for i in range(SIDE)
+    ]
+
+    @pl.when(c == 0)
+    def _():
+        first = edge_pre[1] + mm(edge_pre[0], start[...])
+        for i in range(SIDE):
+            edges[i] = first[8 * i : 8 * i + 8, :] * edge_in[i, 2]
+
+            @pl.when((y > 0) | (place(i) > 0))
+            def _():
+                edge_sends[i].start()
+
     forwards = [
         remote(back.at[h], other.at[h], fwd_s.at[h], fwd_r.at[h], partner) for h in heads
     ]
@@ -342,14 +402,6 @@
                 remote(sends.at[0], back.at[h], back_s.at[0], back_r.at[h], partner).wait_recv()
 
             forwards[h].start()
-
-    def gradients(carries):
-        for h in heads:
-            if carries is other:
-                forwards[h].wait_recv()
-            pg = (lg[h] + mm(wt[h], carries[h])) * dsig[h]
-            pg_pad[h, :N, :] = pg
-            pg_first[h] = pg[:8, :]
 
     def queries(h, state):
         reach = lax.dot_general(
@@ -361,40 +413,88 @@
         weights = pl_mix[h] - jnp.where(t_id >= s_id, mixed, 0.0) * beta_ref[h : h + 1, :]
         qg_ref[h] = e1[h] * mm(weights, kgc[h]) + e0[h] * reach
 
-    pg_copy = remote(pg_first, pg_next, pg_s, pg_r, preceding)
+    def take(own):
+        @pl.when(own)
+        def _():
+            hand_on()
+
+        @pl.when(jnp.logical_not(own))
+        def _():
+            for copy in forwards:
+                copy.wait_recv()
+
+    def query_side():
+        take(c == 1)
+
+        @pl.when(c == 1)
+        def _():
+            for h in heads:
+                queries(h, mm(pair[h, 0], back[h]) + pair[h, 1])
+
+        @pl.when(c == 0)
+        def _():
+            for h in heads:
+                queries(h, other[h])
+
+    def input_side():
+        take(c == 0)
+
+        @pl.when(c == 0)
+        def _():
+            near_copy.wait_recv()
+            for h in heads:
+                other_edge = near[h, 1] + mm(near[h, 0], back[h])
+                pg_pad[h, N:, :] = other_edge * near[h, 2]
+                pg_pad[h, :N, :] = (lg[h] + mm(wt[h], back[h])) * dsig[h]
+
+        @pl.when(c == 1)
+        def _():
+            for h in heads:
+                pg_pad[h, :N, :] = (lg[h] + mm(wt[h], other[h])) * dsig[h]
+
+            @pl.when(me == RING - 1)
+            def _():
+                pg_pad[:, N:, :] = jnp.zeros((HEADS, 8, N), F32)
+
+            @pl.when(me < RING - 1)
+            def _():
+                for h in heads:
+                    remote(edges.at[0], pg_next.at[h], pg_s.at[0], pg_r.at[h], partner).wait_recv()
+                    pg_pad[h, N:, :] = pg_next[h]
+
+        for h in heads:
+            grad = w_ref[0, h : h + 1, :] * pg_pad[h, :N, :]
+            for j in range(1, 4):
+                grad = grad + w_ref[j, h : h + 1, :] * pg_pad[h, j : j + N, :]
+            ig_ref[h] = grad
+
+    queries_first = (y == 0) | ((c == 1) & (y < SIDE - 1))
+
+    @pl.when(queries_first)
+    def _():
+        query_side()
+        input_side()
+
+    @pl.when(jnp.logical_not(queries_first))
+    def _():
+        input_side()
+        query_side()
 
     @pl.when(c == 0)
     def _():
-        hand_on()
-        gradients(back)
-        pg_copy.start()
-        for h in heads:
-            forwards[h].wait_recv()
-            queries(h, other[h])
+        for copy in edge_copies:
+            copy.wait_send()
+        for i in range(SIDE):
+            @pl.when((y > 0) | (place(i) > 0))
+            def _():
+                edge_sends[i].wait_send()
 
     @pl.when(c == 1)
     def _():
-        hand_on()
-        for h in heads:
-            queries(h, mm(pair[h, 0], back[h]) + pair[h, 1])
-        gradients(other)
-        pg_copy.start()
-
-    pending += [pg_copy.wait_send] + [copy.wait_send for copy in forwards]
-    body = N - 8
-
-    def mixed_rows(h, first, count):
-        grad = w_ref[0, h : h + 1, :] * pg_pad[h, first : first + count, :]
-        for j in range(1, 4):
-            grad = grad + w_ref[j, h : h + 1, :] * pg_pad[h, first + j : first + j + count, :]
-        ig_ref[h, first : first + count, :] = grad
-
-    for h in heads:
-        mixed_rows(h, 0, body)
-    pg_copy.wait_recv()
-    for h in heads:
-        pg_pad[h, N:, :] = jnp.where(me < RING - 1, pg_next[h], 0.0)
-        mixed_rows(h, body, 8)
+        near_copy.wait_send()
+
+    for copy in forwards:
+        copy.wait_send()
     for wait in pending:
         wait()
 
@@ -455,7 +555,11 @@
             square(HEADS),
             square(HEADS),
             square(HEADS),
-            pltpu.VMEM((HEADS, 8, N), F32),
+            pltpu.VMEM((HEADS, 3, 8, N), F32),
+            pltpu.VMEM((SIDE, 3, 8, N), F32),
+            pltpu.VMEM((2, 8 * SIDE, N), F32),
+            pltpu.VMEM((SIDE, 8, N), F32),
+            pltpu.VMEM((HEADS, 3, 8, N), F32),
             pltpu.VMEM((HEADS, 8, N), F32),
             pltpu.VMEM((HEADS, N + 8, N), F32),
             sem((7,)),
@@ -465,6 +569,8 @@
             sem((SIDE, 2)), sem((SIDE, 2)),
             sem((SIDE,)), sem((HEADS,)),
             sem((HEADS,)), sem((HEADS,)),
+            sem((SIDE,)), sem((HEADS,)),
+            sem((SIDE,)), sem((SIDE,)),
             sem, sem,
         ],
         compiler_params=pltpu.CompilerParams(

time: 35.2 us -> 34.9 us (level)
  Pallas kernels: 34.5 us -> 34.1 us
    pallas_call x1, Pallas kernels: 33.6 us -> 33.3 us  [local(): pl.pallas_call(kernel, out_shape=(pltpu.VMEM((HEADS, N, N), F32),) * 2, i...]
where the time goes in v3:
time: 34.9 us; the launch traced here: 34.8 us
  Pallas kernels  34.1 us (98%)
  between operations  0.64 us (2%)
    pallas_call x1, Pallas kernels, local(): pl.pallas_call(kernel, out_shape=(pltpu.VMEM((HEADS, N, N), F32),) * 2, i...  33.3 us
    pallas_call x1, Pallas kernels, local(): pl.pallas_call(deliver, out_shape=(out, out), in_specs=[vmem] * 2, out_sp...  0.85 us

profile of v3, /device:TPU:1, one launch (start us, length us, event | category | flops | bytes accessed | tf_op | source)
XLA Modules:
  0.0 34.8 jit_solution(540217732861311243)
XLA Ops:
  0.6 33.3 %delta_backward.1 = (f32[4,128,128]{2,1,0:T(8,128)S(1)}, f32[4,128,128]{2,1,0:T(8,128)S(1)}) custom-call(bf16[4,128,128]{2,1,0:T(8,128)(2,1)} %q_hbm.1, bf16[4,128,128]{2,1,0:T(8,128)(2,1)} %k_hbm.1, bf16[4,128,128]{2,1,0:T(8,128)(2,1)} %v_hbm.1, bf16[4,128,128]{2,1,0:T(8,128)(2,1)} %o_hbm.1, f32[4,128,128]{2,1,0:T(8,128)} %g_hbm.1, f32[4,128]{1,0:T(4,128)} %beta_hbm.1, ...), custom_call_target="tpu_custom_call" | custom-call | tf_op jit(solution)/shard_map/delta_backward/pallas_call | solution.py:520
  33.9 0.9 %deliver.1 = (f32[4,128,128]{2,1,0:T(8,128)}, f32[4,128,128]{2,1,0:T(8,128)}) custom-call(f32[4,128,128]{2,1,0:T(8,128)S(1)} %get-tuple-element.4.qg_from, f32[4,128,128]{2,1,0:T(8,128)S(1)} %get-tuple-element.5.ig_from), custom_call_target="tpu_custom_call" | custom-call | tf_op jit(solution)/shard_map/deliver/pallas_call | solution.py:581

commit v4 on v3

--- a/solution.py
+++ b/solution.py
@@ -129,11 +129,13 @@
         return (t_id // large == s_id // large) & (t_id // small > s_id // small)
 
     heads = range(HEADS)
-    system, kd_all, ket_all, kdt_all, qto_all, keep_all, beta_col_all, qn_all = [[] for _ in range(8)]
+    order = [lax.rem(x + d, SIDE) for d in (2, 1, 3, 0)]
+    held = [{} for _ in order]
     for load in loads[:3]:
         load.wait()
-    since_all, full_all = [], []
-    for h in heads:
+
+    def prepare(i):
+        h, mine = order[i], held[i]
         k = k_ref[h].astype(F32)
         k = k * lax.rsqrt(jnp.sum(k * k, axis=1, keepdims=True) + 1e-6)
         g = g_ref[h]
@@ -153,86 +155,97 @@
         to_end = until * jnp.exp(last - middle)
         e1[h] = since
         e0[h] = full
-        beta_row = beta_ref[h : h + 1, :]
+        beta_row = beta_ref[pl.ds(h, 1), :]
         k_until = k * until
         kgc[h] = k_until
         mix = mm_t(k * since, k_until)
-        system.append(jnp.where(t_id > s_id, mix * beta_row, 0.0))
-        beta_col_all.append(jnp.sum(eye * beta_row, axis=1, keepdims=True))
-        kd_all.append(k * full)
-        qn_all.append(k * to_end)
-        since_all.append(since)
-        full_all.append(full)
-        keep_all.append(jnp.exp(last))
-
+        mine["system"] = jnp.where(t_id > s_id, mix * beta_row, 0.0)
+        mine["beta"] = jnp.sum(eye * beta_row, axis=1, keepdims=True)
+        mine["kd"] = k * full
+        mine["k_end"] = k * to_end
+        mine["keep"] = jnp.exp(last)
+
+    def invert(group):
+        inverse = {i: eye - jnp.where(block_mask(1, 2), held[i]["system"], 0.0) for i in group}
+        for small in (2, 8, 32):
+            mask = block_mask(small, 4 * small)
+            for i in group:
+                m = mm(inverse[i], jnp.where(mask, held[i]["system"], 0.0))
+                squared, applied = mm(m, m, inverse[i])
+                z = inverse[i] - applied
+                inverse[i] = z + mm(squared, z)
+        for i in group:
+            h, mine = order[i], held[i]
+            mine["inverse"] = inverse[i]
+            inv[h] = inverse[i]
+            mine["ket"] = mine["k_end"].T * beta_ref[pl.ds(h, 1), :]
+            mine["ke"] = mine["k_end"] * mine["beta"]
+            ke[h] = mine["ke"]
+            mine["kdt"] = mine["kd"].T
+            q = q_ref[h].astype(F32)
+            q = q * lax.rsqrt(jnp.sum(q * q, axis=1, keepdims=True) + 1e-6)
+            upper = jnp.where(s_id >= t_id, mm_t(kgc[h], q * e1[h]), 0.0)
+            mine["rhs"] = mine["beta"] * mm_exact(upper, o_ref[h])
+            rhs[h] = mine["rhs"]
+            mine["qto"] = mm_exact((q * e0[h]).T, o_ref[h])
+
+    pair_copies = []
+
+    def finish(i):
+        h, mine = order[i], held[i]
+        padded[h, 8:, :] = v_ref[h].astype(F32)
+        edge = halo_v[h].astype(F32)[8:, :]
+        padded[h, :8, :] = jnp.where(me > 0, edge, 0.0)
+        pre = w_ref[0, pl.ds(h, 1), :] * padded[h, 8:, :]
+        for j in range(1, 4):
+            pre = pre + w_ref[j, pl.ds(h, 1), :] * padded[h, 8 - j : 8 - j + N, :]
+        sig = jax.nn.sigmoid(pre)
+        dsig[h] = sig * (1.0 + pre * (1.0 - sig))
+        value = pre * sig
+        keys_x, values_x = mm(mine["inverse"], mine["kd"], value)
+        keys_xt = mm_t(mine["kdt"], mine["inverse"])
+        fwd_t, fwd_f = mm(mine["ket"], keys_x, values_x)
+        bwd_t, bwd_f = mm(keys_xt, mine["ke"], mine["rhs"])
+        keep = eye * mine["keep"]
+        loc[h, 0, 0] = keep - fwd_t
+        loc[h, 0, 1] = fwd_f
+        loc[h, 1, 0] = keep - bwd_t
+        loc[h, 1, 1] = mine["qto"] - bwd_f
+        xk[h] = keys_x
+        xv[h] = values_x
+        copy = remote(loc.at[h, c], pair.at[h], pair_s.at[h], pair_r.at[h], partner)
+        copy.start()
+        pair_copies.append(copy)
+        pending.append(copy.wait_send)
+
+    def combine(i):
+        h = order[i]
+        pair_copies[i].wait_recv()
+        g_chip, f_chip = mm(loc[h, 1 - c, 0], pair[h, 0], pair[h, 1])
+        if i == SIDE - 1:
+            row[p, 0] = g_chip
+            row[p, 1] = f_chip + loc[h, 1 - c, 1]
+        else:
+            chip[i, 0] = g_chip
+            chip[i, 1] = f_chip + loc[h, 1 - c, 1]
+            copy = remote(chip.at[i], row.at[p], row_s.at[i], row_r.at[p], at(y, h, c))
+            copy.start()
+            pending.append(copy.wait_send)
+
+    for i in range(HEADS):
+        prepare(i)
     pl.semaphore_wait(barrier, len(greeted))
     tail_copy = remote(v_hbm.at[:, N - 16 :, :], halo_v, tail_s, tail_r, following)
     tail_copy.start()
     pending.append(tail_copy.wait_send)
     for load in loads[3:]:
         load.wait()
-
-    inverse = [eye - jnp.where(block_mask(1, 2), system[h], 0.0) for h in heads]
-    for small in (2, 8, 32):
-        mask = block_mask(small, 4 * small)
-        for h in heads:
-            m = mm(inverse[h], jnp.where(mask, system[h], 0.0))
-            squared, applied = mm(m, m, inverse[h])
-            z = inverse[h] - applied
-            inverse[h] = z + mm(squared, z)
-    for h in heads:
-        inv[h] = inverse[h]
-        k_end = qn_all[h]
-        ket_all.append(k_end.T * beta_ref[h : h + 1, :])
-        ke[h] = k_end * beta_col_all[h]
-        kdt_all.append(kd_all[h].T)
-        q = q_ref[h].astype(F32)
-        q = q * lax.rsqrt(jnp.sum(q * q, axis=1, keepdims=True) + 1e-6)
-        upper = jnp.where(s_id >= t_id, mm_t(kgc[h], q * since_all[h]), 0.0)
-        rhs[h] = beta_col_all[h] * mm_exact(upper, o_ref[h])
-        qto_all.append(mm_exact((q * full_all[h]).T, o_ref[h]))
-
+    invert(range(HEADS))
     tail_copy.wait_recv()
-    pair_copies = []
-    for h in heads:
-        padded[h, 8:, :] = v_ref[h].astype(F32)
-        edge = halo_v[h].astype(F32)[8:, :]
-        padded[h, :8, :] = jnp.where(me > 0, edge, 0.0)
-        pre = w_ref[0, h : h + 1, :] * padded[h, 8:, :]
-        for j in range(1, 4):
-            pre = pre + w_ref[j, h : h + 1, :] * padded[h, 8 - j : 8 - j + N, :]
-        sig = jax.nn.sigmoid(pre)
-        dsig[h] = sig * (1.0 + pre * (1.0 - sig))
-        value = pre * sig
-        keys_x, values_x = mm(inverse[h], kd_all[h], value)
-        keys_xt = mm_t(kdt_all[h], inverse[h])
-        fwd_t, fwd_f = mm(ket_all[h], keys_x, values_x)
-        bwd_t, bwd_f = mm(keys_xt, ke[h], rhs[h])
-        keep = eye * keep_all[h]
-        loc[h, 0, 0] = keep - fwd_t
-        loc[h, 0, 1] = fwd_f
-        loc[h, 1, 0] = keep - bwd_t
-        loc[h, 1, 1] = qto_all[h] - bwd_f
-        xk[h] = keys_x
-        xv[h] = values_x
-        copy = remote(loc.at[h, c], pair.at[h], pair_s.at[h], pair_r.at[h], partner)
-        copy.start()
-        pair_copies.append(copy)
-        pending.append(copy.wait_send)
-
-    for d in (2, 1, 3, 0):
-        h = lax.rem(x + d, SIDE)
-        remote(loc.at[h, c], pair.at[h], pair_s.at[h], pair_r.at[h], partner).wait_recv()
-        g_chip, f_chip = mm(loc[h, 1 - c, 0], pair[h, 0], pair[h, 1])
-        if d == 0:
-            row[p, 0] = g_chip
-            row[p, 1] = f_chip + loc[h, 1 - c, 1]
-        else:
-            chip[d, 0] = g_chip
-            chip[d, 1] = f_chip + loc[h, 1 - c, 1]
-            copy = remote(chip.at[d], row.at[p], row_s.at[d], row_r.at[p], at(y, h, c))
-            copy.start()
-            pending.append(copy.wait_send)
+    for i in range(HEADS):
+        finish(i)
+    for i in range(HEADS):
+        combine(i)
 
     for h in heads:
         out_values = lax.dot_general(
@@ -290,7 +303,7 @@
             at(place(target), x, c),
         )
 
-    for target in range(1, SIDE):
+    for target in reversed(range(1, SIDE)):
         @pl.when(r < target)
         def _():
             up(1, target).start()

time: 34.9 us -> 33.8 us (0.968)
  Pallas kernels: 34.1 us -> 33.1 us
    pallas_call x1, Pallas kernels: 33.3 us -> 32.2 us  [local(): pl.pallas_call(kernel, out_shape=(pltpu.VMEM((HEADS, N, N), F32),) * 2, i...]
where the time goes in v4:
time: 33.8 us; the launch traced here: 33.7 us
  Pallas kernels  33.1 us (98%)
  between operations  0.64 us (2%)
    pallas_call x1, Pallas kernels, local(): pl.pallas_call(kernel, out_shape=(pltpu.VMEM((HEADS, N, N), F32),) * 2, i...  32.2 us
    pallas_call x1, Pallas kernels, local(): pl.pallas_call(deliver, out_shape=(out, out), in_specs=[vmem] * 2, out_sp...  0.85 us

profile of v4, /device:TPU:1, one launch (start us, length us, event | category | flops | bytes accessed | tf_op | source)
XLA Modules:
  0.0 33.7 jit_solution(9630484037225559330)
XLA Ops:
  0.6 32.2 %delta_backward.1 = (f32[4,128,128]{2,1,0:T(8,128)S(1)}, f32[4,128,128]{2,1,0:T(8,128)S(1)}) custom-call(bf16[4,128,128]{2,1,0:T(8,128)(2,1)} %q_hbm.1, bf16[4,128,128]{2,1,0:T(8,128)(2,1)} %k_hbm.1, bf16[4,128,128]{2,1,0:T(8,128)(2,1)} %v_hbm.1, bf16[4,128,128]{2,1,0:T(8,128)(2,1)} %o_hbm.1, f32[4,128,128]{2,1,0:T(8,128)} %g_hbm.1, f32[4,128]{1,0:T(4,128)} %beta_hbm.1, ...), custom_call_target="tpu_custom_call" | custom-call | tf_op jit(solution)/shard_map/delta_backward/pallas_call | solution.py:533
  32.8 0.9 %deliver.1 = (f32[4,128,128]{2,1,0:T(8,128)}, f32[4,128,128]{2,1,0:T(8,128)}) custom-call(f32[4,128,128]{2,1,0:T(8,128)S(1)} %get-tuple-element.4.qg_from, f32[4,128,128]{2,1,0:T(8,128)S(1)} %get-tuple-element.5.ig_from), custom_call_target="tpu_custom_call" | custom-call | tf_op jit(solution)/shard_map/deliver/pallas_call | solution.py:594

commit v5 on v4

--- a/solution.py
+++ b/solution.py
@@ -324,12 +324,12 @@
         pending.append(drain)
 
     p3, o3 = mm(row[2, 0], p2, o2)
-    pref[0, 0] = row[0, 0]
-    pref[0, 1] = row[0, 1]
-    pref[1, 0] = p2
-    pref[1, 1] = o2
-    pref[2, 0] = p3
-    pref[2, 1] = o3 + row[2, 1]
+    pref[0] = row[0]
+    pref[1] = row[0]
+    pref[2, 0] = p2
+    pref[2, 1] = o2
+    pref[3, 0] = p3
+    pref[3, 1] = o3 + row[2, 1]
 
     @pl.when(c == 0)
     def _():
@@ -341,7 +341,7 @@
         edge_pre[0, :8, :] = edge_in[0, 0]
         edge_pre[1, :8, :] = edge_in[0, 1]
         for i in range(1, SIDE):
-            through, extra = mm(edge_in[i, 0], pref[i - 1, 0], pref[i - 1, 1])
+            through, extra = mm(edge_in[i, 0], pref[i, 0], pref[i, 1])
             edge_pre[0, 8 * i : 8 * i + 8, :] = through
             edge_pre[1, 8 * i : 8 * i + 8, :] = extra + edge_in[i, 1]
 
@@ -364,30 +364,19 @@
             got(source, 1)
             start[...] = mm(above[source, 0], start[...]) + above[source, 1]
 
-    for target in range(SIDE):
-        if target == 0:
-            sends[0] = start[...]
+    state = start[...]
+    for d in (2, 1, 3, 0):
+        to = lax.rem(x + d, SIDE)
+        slot = place(to)
+        later = mm(pref[slot, 0], state) + pref[slot, 1]
+        there = jnp.where(slot == 0, state, later)
+        if d == 0:
+            back[x] = there
         else:
-            sends[target] = mm(pref[target - 1, 0], start[...]) + pref[target - 1, 1]
-        to = place(target)
-        copy = remote(
-            sends.at[target], back.at[x], back_s.at[target], back_r.at[x], at(y, to, c)
-        )
-
-        @pl.when(to != x)
-        def _():
+            sends[d] = there
+            copy = remote(sends.at[d], back.at[x], back_s.at[d], back_r.at[x], at(y, to, c))
             copy.start()
-
-        @pl.when(to == x)
-        def _():
-            back[x] = sends[target]
-
-        def drain(to=to, copy=copy):
-            @pl.when(to != x)
-            def _():
-                copy.wait_send()
-
-        pending.append(drain)
+            pending.append(copy.wait_send)
 
     edge_sends = [
         remote(edges.at[i], pg_next.at[x], pg_s.at[i], pg_r.at[x], (before(place(i)), head))
@@ -409,12 +398,11 @@
     ]
 
     def hand_on():
-        for h in heads:
-            @pl.when(x != h)
-            def _():
+        for d in (0, 1, 3, 2):
+            h = lax.rem(x + d, SIDE)
+            if d > 0:
                 remote(sends.at[0], back.at[h], back_s.at[0], back_r.at[h], partner).wait_recv()
-
-            forwards[h].start()
+            remote(back.at[h], other.at[h], fwd_s.at[h], fwd_r.at[h], partner).start()
 
     def queries(h, state):
         reach = lax.dot_general(
@@ -552,7 +540,7 @@
             square(SIDE, 2),
             square(2),
             square(SIDE - 1, 2),
-            square(SIDE - 1, 2),
+            square(SIDE, 2),
             square(),
             square(SIDE),
             square(HEADS),

time: 33.8 us -> 33.3 us (0.985)
  Pallas kernels: 33.1 us -> 32.6 us
    pallas_call x1, Pallas kernels: 32.2 us -> 31.7 us  [local(): pl.pallas_call(kernel, out_shape=(pltpu.VMEM((HEADS, N, N), F32),) * 2, i...]
where the time goes in v5:
time: 33.3 us; the launch traced here: 33.2 us
  Pallas kernels  32.6 us (98%)
  between operations  0.64 us (2%)
    pallas_call x1, Pallas kernels, local(): pl.pallas_call(kernel, out_shape=(pltpu.VMEM((HEADS, N, N), F32),) * 2, i...  31.7 us
    pallas_call x1, Pallas kernels, local(): pl.pallas_call(deliver, out_shape=(out, out), in_specs=[vmem] * 2, out_sp...  0.85 us

profile of v5, /device:TPU:1, one launch (start us, length us, event | category | flops | bytes accessed | tf_op | source)
XLA Modules:
  0.0 33.2 jit_solution(9411892323333105401)
XLA Ops:
  0.6 31.7 %delta_backward.1 = (f32[4,128,128]{2,1,0:T(8,128)S(1)}, f32[4,128,128]{2,1,0:T(8,128)S(1)}) custom-call(bf16[4,128,128]{2,1,0:T(8,128)(2,1)} %q_hbm.1, bf16[4,128,128]{2,1,0:T(8,128)(2,1)} %k_hbm.1, bf16[4,128,128]{2,1,0:T(8,128)(2,1)} %v_hbm.1, bf16[4,128,128]{2,1,0:T(8,128)(2,1)} %o_hbm.1, f32[4,128,128]{2,1,0:T(8,128)} %g_hbm.1, f32[4,128]{1,0:T(4,128)} %beta_hbm.1, ...), custom_call_target="tpu_custom_call" | custom-call | tf_op jit(solution)/shard_map/delta_backward/pallas_call | solution.py:521
  32.4 0.9 %deliver.1 = (f32[4,128,128]{2,1,0:T(8,128)}, f32[4,128,128]{2,1,0:T(8,128)}) custom-call(f32[4,128,128]{2,1,0:T(8,128)S(1)} %get-tuple-element.4.qg_from, f32[4,128,128]{2,1,0:T(8,128)S(1)} %get-tuple-element.5.ig_from), custom_call_target="tpu_custom_call" | custom-call | tf_op jit(solution)/shard_map/deliver/pallas_call | solution.py:582

commit v6 on v5

--- a/solution.py
+++ b/solution.py
@@ -293,9 +293,7 @@
     o2 = o2 + row[1, 1]
     q2, r2 = mm(row[3, 0], row[2, 0], row[2, 1])
     r2 = r2 + row[3, 1]
-    tg, tf = mm(q2, p2, o2)
-    tot[0] = tg
-    tot[1] = tf + r2
+    tot[1] = mm(q2, o2) + r2
 
     def up(kind, target):
         return remote(
@@ -308,6 +306,8 @@
         def _():
             up(1, target).start()
 
+    tot[0] = mm(q2, p2)
+    for target in reversed(range(1, SIDE)):
         @pl.when((r < target) & (r > 0))
         def _():
             up(0, target).start()

time: 33.3 us -> 33.3 us (level)
  no operation moved by 1% of the time
where the time goes in v6:
time: 33.3 us; the launch traced here: 33.2 us
  Pallas kernels  32.6 us (98%)
  between operations  0.64 us (2%)
    pallas_call x1, Pallas kernels, local(): pl.pallas_call(kernel, out_shape=(pltpu.VMEM((HEADS, N, N), F32),) * 2, i...  31.7 us
    pallas_call x1, Pallas kernels, local(): pl.pallas_call(deliver, out_shape=(out, out), in_specs=[vmem] * 2, out_sp...  0.85 us

profile of v6, /device:TPU:1, one launch (start us, length us, event | category | flops | bytes accessed | tf_op | source)
XLA Modules:
  0.0 33.2 jit_solution(7254800339081990940)
XLA Ops:
  0.6 31.7 %delta_backward.1 = (f32[4,128,128]{2,1,0:T(8,128)S(1)}, f32[4,128,128]{2,1,0:T(8,128)S(1)}) custom-call(bf16[4,128,128]{2,1,0:T(8,128)(2,1)} %q_hbm.1, bf16[4,128,128]{2,1,0:T(8,128)(2,1)} %k_hbm.1, bf16[4,128,128]{2,1,0:T(8,128)(2,1)} %v_hbm.1, bf16[4,128,128]{2,1,0:T(8,128)(2,1)} %o_hbm.1, f32[4,128,128]{2,1,0:T(8,128)} %g_hbm.1, f32[4,128]{1,0:T(4,128)} %beta_hbm.1, ...), custom_call_target="tpu_custom_call" | custom-call | tf_op jit(solution)/shard_map/delta_backward/pallas_call | solution.py:521
  32.4 0.9 %deliver.1 = (f32[4,128,128]{2,1,0:T(8,128)}, f32[4,128,128]{2,1,0:T(8,128)}) custom-call(f32[4,128,128]{2,1,0:T(8,128)S(1)} %get-tuple-element.4.qg_from, f32[4,128,128]{2,1,0:T(8,128)S(1)} %get-tuple-element.5.ig_from), custom_call_target="tpu_custom_call" | custom-call | tf_op jit(solution)/shard_map/deliver/pallas_call | solution.py:582
